TPU v7x, 256 devices: a whole 4x4x8 slice. The times are simulated.
256 devices in a mesh: band: 2 (over z_hi), space: 128 (over z_lo, x, y, core).
Axes of the slice: x: 4, y: 4, z: 8 (z_hi: 2, z_lo: 4; z = z_hi * 4 + z_lo), core: 2. Of those that a mesh axis runs over, the one named last changes fastest.
Arguments:
- psi: float32 [32, 128, 8, 8, 128], P('band', 'space'), may hold values from -12 to 12
- potential: float32 [128, 8, 8, 128], P('space'), may hold values from -3 to 0
- projector: float32 [128, 32, 16, 128], P('space'), may hold values from -0.5 to 0.5
- coupling: float32 [128, 32, 16], P('space'), may hold values from 0.5 to 4
- slot_live: int32 [128], P('space'), may hold values from 0 to 32, as said below
- point_count: int32 [128, 32], P('space'), may hold values from 64 to 128, as said below
- point_index: int32 [128, 32, 128], P('space'), may hold values from 0 to 8191, as said below
Outputs:
- filtered: float32 [32, 128, 8, 8, 128], P('band', 'space')
- gram: float32 [32, 32], P('band')
Inputs may be any that keep to these rules, and one draw needn't show every extreme that they name: `slot_live`: tiles 128 // 2 and above (the vacuum half along the first grid dimension) own no atoms; some tile owns exactly 32. `point_count`: slot 0 of every tile uses all 128 points. `point_index`: cells of the slot's own tile near an atom centre; cells may repeat.
All inputs are finite; a program needn't handle non-finite values.
Results may differ from a plain program's by a relative error of at most 0.0001.
Values sent between devices are 32-bit elements; how exact they have to be, the bound alone decides.
A program may use at most 192 MiB of HBM per device.

v0:
```python
import jax
import jax.numpy as jnp
from jax import lax
from jax.sharding import PartitionSpec as P

LAP_COEFFS = (
    -5369.0 / 1800.0,
    12.0 / 7.0,
    -15.0 / 56.0,
    10.0 / 189.0,
    -1.0 / 112.0,
    2.0 / 1925.0,
    -1.0 / 16632.0,
)
KINETIC = -2.0
FILTERS = ((10.0, 60.0, -2.0), (6.0, 60.0, -2.0))
WIDTH = 6


def passed_along(block, axis, distance):
    devices = range(lax.axis_size(axis))
    route = [((i - distance) % len(devices), i) for i in devices]
    return lax.ppermute(block, axis, route)


def swapped(value, axis, stride):
    mask = 2**stride
    pairs = [(source, source ^ mask) for source in range(lax.axis_size(axis))]
    return lax.ppermute(value, axis, pairs)


def projector_weights(projector, point_count, slot_live):
    points = lax.broadcasted_iota(jnp.int32, projector.shape, projector.ndim - 1)
    slots = lax.broadcasted_iota(jnp.int32, projector.shape, projector.ndim - 3)
    keep = (points < point_count[..., None, None]) & (slots < slot_live[..., None, None, None])
    return jnp.where(keep, projector, jnp.zeros_like(projector))


def from_tile(piece, offset):
    return passed_along(piece, "space", offset)


def depth_padded(field):
    span_z = field.shape[3]
    return jnp.concatenate(
        [field[:, :, :, span_z - WIDTH :], field, field[:, :, :, :WIDTH]], axis=3
    )


def laplacian(field):
    span_x = field.shape[1]
    span_y = field.shape[2]
    span_z = field.shape[3]
    lower = from_tile(field[:, span_x - WIDTH :], 2)
    upper = from_tile(field[:, :WIDTH], -2)
    extended_x = jnp.concatenate([lower, field, upper], axis=1)
    sides = jnp.stack([field[:, :, :WIDTH], field[:, :, span_y - WIDTH :]])
    paired = swapped(sides, "space", 0)
    extended_y = jnp.concatenate([paired[1], field, paired[0]], axis=2)
    extended_z = depth_padded(field)
    lap = 3.0 * LAP_COEFFS[0] * field
    for shift in range(1, 7):
        total = (
            extended_x[:, WIDTH + shift : WIDTH + shift + span_x]
            + extended_x[:, WIDTH - shift : WIDTH - shift + span_x]
        )
        total = (
            total
            + extended_y[:, :, WIDTH + shift : WIDTH + shift + span_y]
            + extended_y[:, :, WIDTH - shift : WIDTH - shift + span_y]
        )
        total = (
            total
            + extended_z[:, :, :, WIDTH - shift : WIDTH - shift + span_z]
            + extended_z[:, :, :, WIDTH + shift : WIDTH + shift + span_z]
        )
        lap = lap + LAP_COEFFS[shift] * total
    return lap


def own_nonlocal(field, weights, couple, flat_index):
    band_rows = field.shape[0]
    slots = weights.shape[0]
    flat = field.reshape(band_rows, -1)
    values = jnp.take(flat, flat_index, axis=1).reshape(band_rows, slots, -1)
    coef = jnp.einsum("sjp,bsp->bsj", weights, values, precision=lax.Precision.HIGHEST)
    scaled = coef * couple[None]
    contrib = jnp.einsum("sjp,bsj->bsp", weights, scaled, precision=lax.Precision.HIGHEST)
    added = jnp.zeros_like(flat).at[:, flat_index].add(contrib.reshape(band_rows, -1))
    return added.reshape(field.shape)


def filter_pass(block, cuts, apply_ham):
    low, high, bottom = cuts
    half = (high - low) / 2.0
    centre = (high + low) / 2.0
    sigma = half / (bottom - centre)
    tau = 2.0 / sigma
    older = block
    newer = (apply_ham(block) - centre * block) * (sigma / half)
    sigma_next = 1.0 / (tau - sigma)
    following = (apply_ham(newer) - centre * newer) * (
        2.0 * sigma_next / half
    ) - sigma * sigma_next * older
    older, newer, sigma = (newer, following, sigma_next)
    return newer


def per_device(psi, potential, projector, coupling, slot_live, point_count, point_index):
    weights = projector_weights(projector, point_count, slot_live)[0]
    couple = coupling[0]
    flat_index = point_index[0].reshape(-1)
    local_pot = potential[0]
    field_start = psi[:, 0]
    band_rows = field_start.shape[0]

    def nonlocal_term(field):
        return own_nonlocal(field, weights, couple, flat_index)

    def apply_ham(field):
        return KINETIC * laplacian(field) + local_pot[None] * field + nonlocal_term(field)

    first = filter_pass(field_start, FILTERS[0], apply_ham)
    filtered = filter_pass(first, FILTERS[1], apply_ham)
    flat_out = filtered.reshape(band_rows, -1)
    cells = flat_out.shape[1]
    partial_rows = lax.dot_general(
        flat_out,
        lax.all_gather(flat_out, "band", axis=0, tiled=True),
        (((1,), (1,)), ((), ())),
        precision=lax.Precision.HIGHEST,
        preferred_element_type=jnp.float32,
    )
    rows_here = lax.psum(partial_rows, "space")
    gram = rows_here / (lax.axis_size("space") * cells)
    return (filtered[:, None], gram)


def solution(mesh):
    placed = (
        P("band", "space", None, None, None),
        P("space", None, None, None),
        P("space", None, None, None),
        P("space", None, None),
        P("space"),
        P("space", None),
        P("space", None, None),
    )
    return jax.shard_map(
        per_device,
        mesh=mesh,
        in_specs=placed,
        out_specs=(P("band", "space", None, None, None), P("band", None)),
        check_vma=False,
    )
```

profile of v0, /device:TPU:1, one launch (start us, length us, event | category | flops | bytes accessed | tf_op | source)
XLA Modules:
  0.0 710.1 jit_solution(5858643609258552892)
XLA Ops:
  7.2 1.1 copy.107
  8.4 0.9 pad_maximum_fusion
  9.4 3.2 collective-permute-start.2
  12.6 1.1 fusion.348
  13.7 7.5 %collective-permute-start = (f32[16,6,8,128]{3,1,2,0:T(8,128)}, f32[16,6,8,128]{3,1,2,0:T(8,128)}, u32[]{:S(2)}, u32[]{:S(2)}) collective-permute-start(f32[16,6,8,128]{3,1,2,0:T(8,128)} %get-tuple-element.37), channel_id=1, source_target_pairs={{2,0},{3,1},{4,2},{5,3},{6,4},{7,5},{8,6},{9,7},{10,8},{11,9},{12,... | collective-permute-start | bytes 1179656 | tf_op jit(solution)/shard_map/ppermute | solution.py:23
  21.2 2.6 copy.63
  24.6 16.3 %gather_fusion = f32[4096,16]{1,0:T(8,128)} fusion(f32[16,8192]{0,1:T(8,128)} %bitcast.164, s32[4096]{0:T(1024)S(1)} %fusion.330), kind=kCustom, calls=%fused_computation.clone | custom fusion | bytes 540672 | tf_op jit(solution)/shard_map/jit(_take)/gather | solution.py:85
  40.9 3.6 broadcast_select_fusion.3
  44.6 3.5 fusion.11
  48.5 2.0 copy.67
  50.5 25.0 %scatter_custom_fusion = f32[16,8192]{0,1:T(8,128)} fusion(s32[4096]{0:T(1024)S(1)} %bitcast.190, f32[4096,16]{1,0:T(8,128)} %copy.67, f32[]{:T(128)} %constant.13.clone.1), kind=kCustom, calls=%fused_computation.14 | custom fusion | flops 65536 | bytes 524800 | tf_op jit(solution)/shard_map/scatter-add | solution.py:89
  75.5 2.9 copy.68
  78.7 6.9 broadcast_multiply_fusion.1
  85.7 2.7 copy.70
  88.4 16.3 %gather_fusion.1 = f32[4096,16]{1,0:T(8,128)} fusion(f32[16,8192]{0,1:T(8,128)} %bitcast.166, s32[4096]{0:T(1024)S(1)} %fusion.330), kind=kCustom, calls=%fused_computation.1.clone | custom fusion | bytes 540672 | tf_op jit(solution)/shard_map/jit(_take)/gather | solution.py:85
  104.7 3.6 broadcast_select_fusion.2
  109.8 3.5 fusion.10
  113.7 2.0 copy.73
  115.7 24.8 %scatter_custom_fusion.1 = f32[16,8192]{0,1:T(8,128)} fusion(s32[4096]{0:T(1024)S(1)} %bitcast.191, f32[4096,16]{1,0:T(8,128)} %copy.73, f32[]{:T(128)} %constant.13.clone.1), kind=kCustom, calls=%fused_computation.12 | custom fusion | flops 65536 | bytes 524800 | tf_op jit(solution)/shard_map/scatter-add | solution.py:89
  140.5 2.9 copy.74
  143.6 7.7 %collective-permute-start.3 = (f32[16,6,8,128]{3,1,2,0:T(8,128)S(1)}, f32[16,6,8,128]{3,1,2,0:T(8,128)S(1)}, u32[]{:S(2)}, u32[]{:S(2)}) collective-permute-start(f32[16,6,8,128]{3,1,2,0:T(8,128)S(1)} %get-tuple-element.31), channel_id=1, source_target_pairs={{2,0},{3,1},{4,2},{5,3},{6,4},{7,5},{8,6},{9,7},{10,8},{11,9},{12,... | collective-permute-start | bytes 1179656 | tf_op jit(solution)/shard_map/ppermute | solution.py:23
  151.4 1.2 slice_bitcast_fusion.9
  152.6 10.5 %collective-permute-done.4 = f32[16,6,8,128]{3,1,2,0:T(8,128)S(1)} collective-permute-done((f32[16,6,8,128]{3,1,2,0:T(8,128)S(1)}, f32[16,6,8,128]{3,1,2,0:T(8,128)S(1)}, u32[]{:S(2)}, u32[]{:S(2)}) %collective-permute-start.4) | collective-permute-done | bytes 393248 | tf_op jit(solution)/shard_map/ppermute | solution.py:23
  163.1 3.3 fusion.116
  166.4 2.7 copy.75
  169.9 13.0 %gather_fusion.2 = f32[4096,16]{1,0:T(8,128)S(1)} fusion(f32[16,8192]{0,1:T(8,128)} %bitcast.167, s32[4096]{0:T(1024)S(1)} %fusion.330), kind=kCustom, calls=%fused_computation.2.clone | custom fusion | bytes 540672 | tf_op jit(solution)/shard_map/jit(_take)/gather | solution.py:85
  182.9 2.1 broadcast_select_fusion.1
  186.7 3.5 fusion.9
  191.3 24.5 %scatter_custom_fusion.2 = f32[16,8192]{0,1:T(8,128)} fusion(s32[4096]{0:T(1024)S(1)} %bitcast.192, f32[4096,16]{1,0:T(8,128)S(1)} %copy.78, f32[]{:T(128)} %constant.13.clone.1), kind=kCustom, calls=%fused_computation.10 | custom fusion | flops 65536 | bytes 524292 | tf_op jit(solution)/shard_map/scatter-add | solution.py:89
  215.8 2.9 copy.79
  218.9 8.1 %collective-permute-start.6 = (f32[16,6,8,128]{3,1,2,0:T(8,128)S(1)}, f32[16,6,8,128]{3,1,2,0:T(8,128)S(1)}, u32[]{:S(2)}, u32[]{:S(2)}) collective-permute-start(f32[16,6,8,128]{3,1,2,0:T(8,128)S(1)} %get-tuple-element.25), channel_id=1, source_target_pairs={{2,0},{3,1},{4,2},{5,3},{6,4},{7,5},{8,6},{9,7},{10,8},{11,9},{12,... | collective-permute-start | bytes 1179656 | tf_op jit(solution)/shard_map/ppermute | solution.py:23
  227.2 1.2 slice_bitcast_fusion.5
  228.4 10.3 %collective-permute-done.7 = f32[16,6,8,128]{3,1,2,0:T(8,128)S(1)} collective-permute-done((f32[16,6,8,128]{3,1,2,0:T(8,128)S(1)}, f32[16,6,8,128]{3,1,2,0:T(8,128)S(1)}, u32[]{:S(2)}, u32[]{:S(2)}) %collective-permute-start.7) | collective-permute-done | bytes 393248 | tf_op jit(solution)/shard_map/ppermute | solution.py:23
  238.7 4.0 broadcast_multiply_fusion
  242.7 2.6 copy.81
  246.3 13.0 %gather_fusion.3 = f32[4096,16]{1,0:T(8,128)S(1)} fusion(f32[16,8192]{0,1:T(8,128)} %bitcast.165, s32[4096]{0:T(1024)S(1)} %fusion.330), kind=kCustom, calls=%fused_computation.3.clone | custom fusion | bytes 540672 | tf_op jit(solution)/shard_map/jit(_take)/gather | solution.py:85
  259.3 2.1 broadcast_select_fusion
  263.1 3.5 fusion.8
  267.6 24.5 %scatter_custom_fusion.3 = f32[16,8192]{0,1:T(8,128)} fusion(s32[4096]{0:T(1024)S(1)} %bitcast.193, f32[4096,16]{1,0:T(8,128)S(1)} %copy.84, f32[]{:T(128)} %constant.13.clone.1), kind=kCustom, calls=%fused_computation.8 | custom fusion | flops 65536 | bytes 524292 | tf_op jit(solution)/shard_map/scatter-add | solution.py:89
  292.1 2.9 copy.85
  295.2 8.2 %collective-permute-start.9 = (f32[16,6,8,128]{3,1,2,0:T(8,128)S(1)}, f32[16,6,8,128]{3,1,2,0:T(8,128)S(1)}, u32[]{:S(2)}, u32[]{:S(2)}) collective-permute-start(f32[16,6,8,128]{3,1,2,0:T(8,128)S(1)} %get-tuple-element.19), channel_id=1, source_target_pairs={{2,0},{3,1},{4,2},{5,3},{6,4},{7,5},{8,6},{9,7},{10,8},{11,9},{12,... | collective-permute-start | bytes 1179656 | tf_op jit(solution)/shard_map/ppermute | solution.py:23
  303.6 1.2 slice_bitcast_fusion.1
  304.8 10.6 %collective-permute-done.10 = f32[16,6,8,128]{3,1,2,0:T(8,128)S(1)} collective-permute-done((f32[16,6,8,128]{3,1,2,0:T(8,128)S(1)}, f32[16,6,8,128]{3,1,2,0:T(8,128)S(1)}, u32[]{:S(2)}, u32[]{:S(2)}) %collective-permute-start.10) | collective-permute-done | bytes 393248 | tf_op jit(solution)/shard_map/ppermute | solution.py:23
  315.5 3.3 fusion.24
  318.9 1.1 copy.106
  320.9 42.0 %all-gather.2.cloned.1.call-done = f32[32,8192]{1,0:T(8,128)} async-done(((f32[16,8192]{1,0:T(8,128)}), f32[32,8192]{1,0:T(8,128)}) %all-gather.2.cloned.1.call-update) | async-done | bytes 1048592 | tf_op jit(solution)/shard_map/all_gather | solution.py:129
  362.9 2.3 fusion.331
  365.2 337.2 %psum.7 = f32[16,32]{1,0:T(8,128)S(1)} all-reduce(f32[16,32]{1,0:T(8,128)S(1)} %fusion.331), channel_id=1, replica_groups=mesh['band'=2,'space'=128] {'space'}, use_global_device_ids=true, to_apply=%region_4.6 | all-reduce | flops 512 | bytes 4096 | tf_op jit(solution)/shard_map/psum | solution.py:134
  (74 shorter events, 12.9 us)
Async XLA Ops:
  7.2 355.7 %all-gather.2.cloned.1.call-start = ((), (), s32[]{:S(2)}) async-start(), calls=%async_computation | async-start | bytes 1572864 | tf_op jit(solution)/shard_map/all_gather | solution.py:129
  8.4 12.8 %copy-start.1 = (f32[16,1,8,8,128]{4,3,2,1,0:T(8,128)S(1)}, f32[16,1,8,8,128]{4,3,2,1,0:T(8,128)}, u32[]{:S(2)}) copy-start(f32[16,1,8,8,128]{4,3,2,1,0:T(8,128)} %param.9) | copy-start | bytes 1572868
  9.4 69.3 %collective-permute-start.2 = (f32[2,16,8,6,128]{4,2,3,1,0:T(8,128)}, f32[2,16,8,6,128]{4,2,3,1,0:T(8,128)S(1)}, u32[]{:S(2)}, u32[]{:S(2)}) collective-permute-start(f32[2,16,8,6,128]{4,2,3,1,0:T(8,128)} %pad_maximum_fusion), channel_id=1, source_target_pairs={{0,1},{1,0},{2,3},{3,2},{4,5},{5,4},{6,7},{7,6},{8,9},{9,8},{10,11... | collective-permute-start | bytes 2359304 | tf_op jit(solution)/shard_map/ppermute | solution.py:29
  13.7 65.0 %collective-permute-start.1 = (f32[16,6,8,128]{3,1,2,0:T(8,128)}, f32[16,6,8,128]{3,1,2,0:T(8,128)}, u32[]{:S(2)}, u32[]{:S(2)}) collective-permute-start(f32[16,6,8,128]{3,1,2,0:T(8,128)} %get-tuple-element.38), channel_id=1, source_target_pairs={{126,0},{127,1},{0,2},{1,3},{2,4},{3,5},{4,6},{5,7},{6,8},{7,9},{8... | collective-permute-start | bytes 1179656 | tf_op jit(solution)/shard_map/ppermute | solution.py:23
  13.7 10.1 %copy-start.6 = (s32[1,32,128]{2,1,0:T(8,128)S(1)}, s32[1,32,128]{2,1,0:T(8,128)}, u32[]{:S(2)}) copy-start(s32[1,32,128]{2,1,0:T(8,128)} %param.15) | copy-start | bytes 49156
  13.7 10.2 %copy-start.9 = (f32[1,32,16]{1,2,0:T(8,128)S(1)}, f32[1,32,16]{1,2,0:T(8,128)}, u32[]{:S(2)}) copy-start(f32[1,32,16]{1,2,0:T(8,128)} %param.12) | copy-start | bytes 6148
  13.7 65.0 %collective-permute-start = (f32[16,6,8,128]{3,1,2,0:T(8,128)}, f32[16,6,8,128]{3,1,2,0:T(8,128)}, u32[]{:S(2)}, u32[]{:S(2)}) collective-permute-start(f32[16,6,8,128]{3,1,2,0:T(8,128)} %get-tuple-element.37), channel_id=1, source_target_pairs={{2,0},{3,1},{4,2},{5,3},{6,4},{7,5},{8,6},{9,7},{10,8},{11,9},{12,... | collective-permute-start | bytes 1179656 | tf_op jit(solution)/shard_map/ppermute | solution.py:23
  40.9 3.7 copy-start
  40.9 3.7 copy-start.8
  75.5 2.9 copy-start.7
  109.2 42.2 %collective-permute-start.5 = (f32[2,16,8,6,128]{4,2,3,1,0:T(8,128)}, f32[2,16,8,6,128]{4,2,3,1,0:T(8,128)}, u32[]{:S(2)}, u32[]{:S(2)}) collective-permute-start(f32[2,16,8,6,128]{4,2,3,1,0:T(8,128)} %pad_maximum_fusion.1), channel_id=1, source_target_pairs={{0,1},{1,0},{2,3},{3,2},{4,5},{5,4},{6,7},{7,6},{8,9},{9,8},{10,11... | collective-permute-start | bytes 2359304 | tf_op jit(solution)/shard_map/ppermute | solution.py:29
  143.5 19.6 %collective-permute-start.4 = (f32[16,6,8,128]{3,1,2,0:T(8,128)S(1)}, f32[16,6,8,128]{3,1,2,0:T(8,128)S(1)}, u32[]{:S(2)}, u32[]{:S(2)}) collective-permute-start(f32[16,6,8,128]{3,1,2,0:T(8,128)S(1)} %get-tuple-element.32), channel_id=1, source_target_pairs={{126,0},{127,1},{0,2},{1,3},{2,4},{3,5},{4,6},{5,7},{6,8},{7,9},{8... | collective-permute-start | bytes 1179656 | tf_op jit(solution)/shard_map/ppermute | solution.py:23
  143.6 19.6 %collective-permute-start.3 = (f32[16,6,8,128]{3,1,2,0:T(8,128)S(1)}, f32[16,6,8,128]{3,1,2,0:T(8,128)S(1)}, u32[]{:S(2)}, u32[]{:S(2)}) collective-permute-start(f32[16,6,8,128]{3,1,2,0:T(8,128)S(1)} %get-tuple-element.31), channel_id=1, source_target_pairs={{2,0},{3,1},{4,2},{5,3},{6,4},{7,5},{8,6},{9,7},{10,8},{11,9},{12,... | collective-permute-start | bytes 1179656 | tf_op jit(solution)/shard_map/ppermute | solution.py:23
  182.9 2.2 copy-start.5
  186.0 41.3 %collective-permute-start.8 = (f32[2,16,8,6,128]{4,2,3,1,0:T(8,128)}, f32[2,16,8,6,128]{4,2,3,1,0:T(8,128)}, u32[]{:S(2)}, u32[]{:S(2)}) collective-permute-start(f32[2,16,8,6,128]{4,2,3,1,0:T(8,128)} %pad_maximum_fusion.2), channel_id=1, source_target_pairs={{0,1},{1,0},{2,3},{3,2},{4,5},{5,4},{6,7},{7,6},{8,9},{9,8},{10,11... | collective-permute-start | bytes 2359304 | tf_op jit(solution)/shard_map/ppermute | solution.py:29
  218.8 20.0 %collective-permute-start.7 = (f32[16,6,8,128]{3,1,2,0:T(8,128)S(1)}, f32[16,6,8,128]{3,1,2,0:T(8,128)S(1)}, u32[]{:S(2)}, u32[]{:S(2)}) collective-permute-start(f32[16,6,8,128]{3,1,2,0:T(8,128)S(1)} %get-tuple-element.26), channel_id=1, source_target_pairs={{126,0},{127,1},{0,2},{1,3},{2,4},{3,5},{4,6},{5,7},{6,8},{7,9},{8... | collective-permute-start | bytes 1179656 | tf_op jit(solution)/shard_map/ppermute | solution.py:23
  218.9 19.9 %collective-permute-start.6 = (f32[16,6,8,128]{3,1,2,0:T(8,128)S(1)}, f32[16,6,8,128]{3,1,2,0:T(8,128)S(1)}, u32[]{:S(2)}, u32[]{:S(2)}) collective-permute-start(f32[16,6,8,128]{3,1,2,0:T(8,128)S(1)} %get-tuple-element.25), channel_id=1, source_target_pairs={{2,0},{3,1},{4,2},{5,3},{6,4},{7,5},{8,6},{9,7},{10,8},{11,9},{12,... | collective-permute-start | bytes 1179656 | tf_op jit(solution)/shard_map/ppermute | solution.py:23
  259.3 2.2 copy-start.3
  259.3 2.2 copy-start.4
  262.4 41.2 %collective-permute-start.11 = (f32[2,16,8,6,128]{4,2,3,1,0:T(8,128)}, f32[2,16,8,6,128]{4,2,3,1,0:T(8,128)}, u32[]{:S(2)}, u32[]{:S(2)}) collective-permute-start(f32[2,16,8,6,128]{4,2,3,1,0:T(8,128)} %pad_maximum_fusion.3), channel_id=1, source_target_pairs={{0,1},{1,0},{2,3},{3,2},{4,5},{5,4},{6,7},{7,6},{8,9},{9,8},{10,11... | collective-permute-start | bytes 2359304 | tf_op jit(solution)/shard_map/ppermute | solution.py:29
  295.1 20.4 %copy-start.2 = (f32[16,8,8,128]{3,1,2,0:T(8,128)S(1)}, f32[16,8,8,128]{3,1,2,0:T(8,128)}, u32[]{:S(2)}) copy-start(f32[16,8,8,128]{3,1,2,0:T(8,128)} %get-tuple-element.8) | copy-start | bytes 1572868
  295.1 20.3 %collective-permute-start.10 = (f32[16,6,8,128]{3,1,2,0:T(8,128)S(1)}, f32[16,6,8,128]{3,1,2,0:T(8,128)S(1)}, u32[]{:S(2)}, u32[]{:S(2)}) collective-permute-start(f32[16,6,8,128]{3,1,2,0:T(8,128)S(1)} %get-tuple-element.20), channel_id=1, source_target_pairs={{126,0},{127,1},{0,2},{1,3},{2,4},{3,5},{4,6},{5,7},{6,8},{7,9},{8... | collective-permute-start | bytes 1179656 | tf_op jit(solution)/shard_map/ppermute | solution.py:23
  295.2 20.3 %collective-permute-start.9 = (f32[16,6,8,128]{3,1,2,0:T(8,128)S(1)}, f32[16,6,8,128]{3,1,2,0:T(8,128)S(1)}, u32[]{:S(2)}, u32[]{:S(2)}) collective-permute-start(f32[16,6,8,128]{3,1,2,0:T(8,128)S(1)} %get-tuple-element.19), channel_id=1, source_target_pairs={{2,0},{3,1},{4,2},{5,3},{6,4},{7,5},{8,6},{9,7},{10,8},{11,9},{12,... | collective-permute-start | bytes 1179656 | tf_op jit(solution)/shard_map/ppermute | solution.py:23
Sparse Core Ops, SparseCore 0:
  320.1 42.7 all-gather.1
where the time goes:
time: 717 us; the launch traced here: 710 us
  blocking collectives  337 us (47%)
  other arithmetic  132 us (18%)
  local copies, waits for them, and re-layouts  96.6 us (13%)
  waiting for transfers between devices  73.5 us (10%)
  starting transfers between devices  37 us (5%)
  matrix products  18 us (3%)
  between operations  15.4 us (2%)
    psum x1, blocking collectives, per_device(): rows_here = lax.psum(partial_rows, 'space')  337 us
    scatter-add x4, other arithmetic, own_nonlocal(): jnp.zeros_like(flat).at[:, flat_index].add(contrib.reshape(band_rows, -1))  98.9 us
    gather x4, local copies, waits for them, and re-layouts, own_nonlocal(): values = jnp.take(flat, flat_index, axis=1).reshape(band_rows, slots, -1)  58.5 us
    all_gather x1, waiting for transfers between devices, per_device(): lax.all_gather(flat_out, 'band', axis=0, tiled=True)  42 us
    ppermute x8, starting transfers between devices, passed_along(): return lax.ppermute(block, axis, route)  31.8 us
    ppermute x8, waiting for transfers between devices, passed_along(): return lax.ppermute(block, axis, route)  31.5 us
  transfers between devices with their start and end apart: 13, of which 4 were waited for; matrix products, arithmetic and copies ran while one was open for 23% of the time, Pallas kernels for 0%

commit v1 on v0

v1 whole, which is shorter than its diff:
```python
import functools

import jax
import jax.numpy as jnp
from jax import lax
from jax.experimental import pallas as pl
from jax.experimental.pallas import tpu as pltpu
from jax.sharding import PartitionSpec as P

LAP_COEFFS = (
    -5369.0 / 1800.0,
    12.0 / 7.0,
    -15.0 / 56.0,
    10.0 / 189.0,
    -1.0 / 112.0,
    2.0 / 1925.0,
    -1.0 / 16632.0,
)
KINETIC = -2.0
FILTERS = ((10.0, 60.0, -2.0), (6.0, 60.0, -2.0))
WIDTH = 6
MESH = pl.DeviceIdType.MESH
F32, BF16 = jnp.float32, jnp.bfloat16

SX, SY, SZ = 8, 8, 128
ROWS = SX * SY
GB = 8
PAIRS = ROWS // 2
SLOTS, NPROJ, PTS = 32, 16, 128
POINTS = SLOTS * PTS
CHUNK = 1024
CHUNK_SLOTS = CHUNK // PTS
STEPS = 4


def step_constants():
    scale, carry, shift = [], [], []
    for low, high, bottom in FILTERS:
        half = (high - low) / 2.0
        centre = (high + low) / 2.0
        sigma = half / (bottom - centre)
        tau = 2.0 / sigma
        following = 1.0 / (tau - sigma)
        scale += [sigma / half, 2.0 * following / half]
        carry += [0.0, -sigma * following]
        shift += [centre, centre]
    return scale, carry, shift


SCALE, CARRY, SHIFT = step_constants()


def chosen(step, values):
    out = jnp.float32(values[-1])
    for at in range(len(values) - 2, -1, -1):
        out = jnp.where(step == at, jnp.float32(values[at]), out)
    return out


def two_parts(value):
    high = value.astype(BF16).astype(F32)
    return jnp.concatenate([high, value - high], axis=0).astype(BF16)


def dot(a, b):
    return jnp.dot(a, b, preferred_element_type=F32)


def dot_t(a, b):
    return lax.dot_general(a, b, (((1,), (1,)), ((), ())), preferred_element_type=F32)


def kernel(
    tiles,
    psi_in,
    pot_in,
    projector_in,
    coupling_in,
    slot_live_in,
    point_count_in,
    point_index_in,
    out,
    gram,
    ready,
    psi,
    pot,
    projector,
    coupling,
    slot_live,
    point_count,
    point_index,
    field,
    low_x,
    high_x,
    other_y,
    other_band,
    hot,
    pair_of,
    pair_of16,
    operator,
    parts,
    added,
    local,
    wide,
    wide_other,
    send,
    recv,
    send_band,
    recv_band,
    sums,
    sums_in,
    send_sums,
    recv_sums,
    load,
):
    groups = field.shape[1]
    band = lax.axis_index("band")
    tile = lax.axis_index("space")
    up = (band, lax.rem(tile + 2, tiles))
    down = (band, lax.rem(tile + tiles - 2, tiles))
    beside = (band, tile + 1 - 2 * lax.rem(tile, 2))
    across = (1 - band, tile)

    def turned_by(span, low, away):
        return (band, tile - lax.rem(tile, span) + lax.rem(lax.rem(tile, span) + away * low, span))

    depth = tiles // 32
    ring = band * depth + tile // 32

    def along(away):
        place = lax.rem(ring + away, 2 * depth)
        return (place // depth, lax.rem(place, depth) * 32 + lax.rem(tile, 32))

    phases = (
        [beside],
        [turned_by(8, 2, away) for away in range(1, 4)],
        [turned_by(32, 8, away) for away in range(1, 4)],
        [along(away) for away in range(1, 2 * depth)],
    )

    barrier = pltpu.get_barrier_semaphore()
    greeted = [up, down] + [device for phase in phases for device in phase]
    for device in greeted:
        pl.semaphore_signal(barrier, inc=1, device_id=device, device_id_type=MESH)

    def loaded(src, dst, at):
        return pltpu.make_async_copy(src, dst, load.at[at])

    loads = [
        loaded(psi_in.at[pl.ds(g * GB, GB)], psi.at[pl.ds(g * GB, GB)], g) for g in range(groups)
    ] + [
        loaded(src, dst, groups + at)
        for at, (src, dst) in enumerate(
            (
                (point_index_in, point_index),
                (projector_in, projector),
                (coupling_in, coupling),
                (slot_live_in, slot_live),
                (point_count_in, point_count),
                (pot_in, pot),
            )
        )
    ]
    for copy in loads:
        copy.start()

    def halo_copies(turn, g):
        def copy(src, dst, which, device):
            return pltpu.make_async_remote_copy(
                src_ref=src,
                dst_ref=dst,
                send_sem=send.at[turn, g, which],
                recv_sem=recv.at[turn, g, which],
                device_id=device,
                device_id_type=MESH,
            )

        edge = WIDTH * SY
        return (
            copy(field.at[turn, g, pl.ds(ROWS - edge, edge)], low_x.at[turn, g], 0, up),
            copy(field.at[turn, g, pl.ds(0, edge)], high_x.at[turn, g], 1, down),
            copy(field.at[turn, g], other_y.at[turn, g], 2, beside),
        )

    def band_copy(g):
        return pltpu.make_async_remote_copy(
            src_ref=field.at[0, g, pl.ds(band * (ROWS // 2), ROWS // 2)],
            dst_ref=other_band.at[g],
            send_sem=send_band.at[g],
            recv_sem=recv_band.at[g],
            device_id=across,
            device_id_type=MESH,
        )

    def split_pair(pair, first, second):
        parts[pair] = two_parts(jnp.concatenate([first, second], axis=1))

    for g in range(groups):
        loads[g].wait()
        for b in range(GB):
            for x in range(SX):
                field[0, g, pl.ds(x * SY, SY), b, :] = psi[g * GB + b, pl.ds(x * SY, SY)]
        if g == 0:
            pl.semaphore_wait(barrier, len(greeted))
        for copy in halo_copies(0, g):
            copy.start()

    field[1] = jnp.zeros(field.shape[1:], F32)
    for copy in loads[groups:]:
        copy.wait()

    @pl.loop(0, SLOTS, unroll=4)
    def _(s):
        cols = pl.ds(pl.multiple_of(s * PTS, PTS), PTS)
        index = point_index[pl.ds(s, 1), :]
        place = jnp.broadcast_to(index & 255, (256, PTS))
        spots = lax.broadcasted_iota(jnp.int32, (256, PTS), 0)
        hot[:, cols] = jnp.where(place == spots, 1.0, 0.0).astype(BF16)
        pair = jnp.broadcast_to(index >> 8, (16, PTS))
        pair_of[:, cols] = pair
        pair_of16[:, cols] = pair.astype(F32).astype(BF16)
        points = lax.broadcasted_iota(jnp.int32, (NPROJ, PTS), 1)
        slots = jnp.full((NPROJ, PTS), s, jnp.int32)
        keep = (points < point_count[s]) & (slots < slot_live[0])
        weights = jnp.where(keep, projector[s], 0.0)
        mine = lax.broadcasted_iota(jnp.int32, (NPROJ, SLOTS), 1) == s
        couple = jnp.sum(jnp.where(mine, coupling[...], 0.0), axis=1, keepdims=True)
        coupled = weights * couple
        weights_high = weights.astype(BF16).astype(F32)
        coupled_high = coupled.astype(BF16).astype(F32)
        left = jnp.concatenate([weights_high, weights_high, weights - weights_high], axis=0)
        right = jnp.concatenate([coupled_high, coupled - coupled_high, coupled_high], axis=0)
        square = dot(left.T.astype(BF16), right.astype(BF16))
        square_high = square.astype(BF16).astype(F32)
        operator[s] = jnp.concatenate([square_high, square - square_high], axis=1).astype(BF16)

    def nonlocal_chunk(g, c):
        cols = pl.ds(c * CHUNK, CHUNK)
        one_hot = hot[:, cols]
        picked = dot(parts[...].reshape(PAIRS * 16, 256), one_hot)
        pairs = pair_of[:, cols]
        values = jnp.zeros((16, CHUNK), F32)
        for pair in range(PAIRS):
            values = jnp.where(pairs == pair, picked[16 * pair : 16 * pair + 16], values)
        values = values[:8] + values[8:]
        given = []
        for s in range(CHUNK_SLOTS):
            product = dot(two_parts(values[:, s * PTS : (s + 1) * PTS]), operator[c * CHUNK_SLOTS + s])
            given.append(
                two_parts(product[:8, :PTS] + (product[:8, PTS:] + product[8:, :PTS]))
            )
        given = jnp.concatenate(given, axis=1)
        pairs = pair_of16[:, cols]
        nothing = jnp.zeros_like(given)
        spread = [jnp.where(pairs == pair, given, nothing) for pair in range(PAIRS)]
        term = dot_t(jnp.concatenate(spread, axis=0), one_hot)
        if c == 0:
            added[g] = term
        else:
            added[g] += term

    def stencil_plane(turn, g, x, diagonal):
        own = [field[turn, g, x * SY + y] for y in range(SY)]
        ring = own + [other_y[turn, g, x * SY + y] for y in range(SY)]
        for y in range(SY):
            value = own[y]
            total = value * (jnp.broadcast_to(pot[pl.ds(x * SY + y, 1)], (GB, SZ)) + diagonal)
            for k in range(1, WIDTH + 1):
                near = ring[(y + k) % (2 * SY)] + ring[(y - k) % (2 * SY)]
                near += pltpu.roll(value, k, axis=1) + pltpu.roll(value, SZ - k, axis=1)
                if x - k >= 0:
                    near += field[turn, g, (x - k) * SY + y]
                if x + k < SX:
                    near += field[turn, g, (x + k) * SY + y]
                total += (KINETIC * LAP_COEFFS[k]) * near
            local[g, x * SY + y] = total

    def apply_local(step, turn, g):
        diagonal = 3.0 * KINETIC * LAP_COEFFS[0] - chosen(step, SHIFT)
        nonlocal_chunk(g, 0)
        nonlocal_chunk(g, 1)
        halo_copies(turn, g)[2].wait_recv()
        nonlocal_chunk(g, 2)
        for x in range(4):
            stencil_plane(turn, g, x, diagonal)
        nonlocal_chunk(g, 3)
        for x in range(4, 8):
            stencil_plane(turn, g, x, diagonal)

    def finish(step, turn, g):
        scale, carry = chosen(step, SCALE), chosen(step, CARRY)
        for y in range(0, SY, 2):
            lower = [[low_x[turn, g, j * SY + y + e] for j in range(WIDTH)] for e in range(2)]
            upper = [[high_x[turn, g, j * SY + y + e] for j in range(WIDTH)] for e in range(2)]
            for x in range(SX):
                pair = x * (SY // 2) + y // 2
                spread = added[g, pl.ds(16 * pair, 16)]
                spread = spread[:8] + spread[8:]
                new = []
                for e in range(2):
                    row = x * SY + y + e
                    total = local[g, row] + spread[:, e * SZ : (e + 1) * SZ]
                    for j in range(WIDTH):
                        if j >= x:
                            total += (KINETIC * LAP_COEFFS[x + WIDTH - j]) * lower[e][j]
                        if j <= x - 2:
                            total += (KINETIC * LAP_COEFFS[SX + j - x]) * upper[e][j]
                    value = scale * total + carry * field[1 - turn, g, row]
                    field[1 - turn, g, row] = value
                    new.append(value)
                split_pair(pair, new[0], new[1])

    for g in range(groups):
        for pair in range(PAIRS):
            split_pair(pair, field[0, g, 2 * pair], field[0, g, 2 * pair + 1])
        apply_local(0, 0, g)

    @pl.loop(0, STEPS * groups)
    def _(at):
        step = at // groups
        g = lax.rem(at, groups)
        turn = lax.rem(step, 2)
        copies = halo_copies(turn, g)
        copies[0].wait()
        copies[1].wait()
        copies[2].wait_send()
        finish(step, turn, g)

        @pl.when(step < STEPS - 1)
        def _():
            for copy in halo_copies(1 - turn, g):
                copy.start()
            apply_local(step + 1, 1 - turn, g)

        @pl.when(step == STEPS - 1)
        def _():
            band_copy(g).start()

    bands = groups * GB
    for g in range(groups):
        for b in range(GB):
            for x in range(SX):
                ready[g * GB + b, pl.ds(x * SY, SY)] = field[0, g, pl.ds(x * SY, SY), b, :]
    store = loaded(ready, out, groups)
    store.start()

    @pl.loop(0, ROWS, unroll=8)
    def _(row):
        cols = pl.ds(pl.multiple_of(row * SZ, SZ), SZ)
        wide[:, cols] = two_parts(jnp.concatenate([field[0, g, row] for g in range(groups)], axis=0))

    def folded(product):
        return (product[:bands, :bands] + product[bands:, bands:]) + (
            product[:bands, bands:] + product[bands:, :bands]
        )

    block = wide[...]
    sums[0, :, :bands] = folded(dot_t(block, block))
    for g in range(groups):
        band_copy(g).wait()

    @pl.loop(0, ROWS // 2, unroll=8)
    def _(row):
        cols = pl.ds(pl.multiple_of(row * SZ, SZ), SZ)
        wide_other[:, cols] = two_parts(
            jnp.concatenate([other_band[g, row] for g in range(groups)], axis=0)
        )

    half = ROWS // 2 * SZ
    kept = wide[:, pl.ds(pl.multiple_of((1 - band) * half, half), half)]
    came = wide_other[...]
    sums[0, :, bands : 2 * bands] = folded(dot_t(kept, came))
    sums[0, :, 2 * bands : 3 * bands] = folded(dot_t(came, kept))

    used = 0
    for at, phase in enumerate(phases):
        copies = []
        for device in phase:
            copies.append(
                pltpu.make_async_remote_copy(
                    src_ref=sums.at[at],
                    dst_ref=sums_in.at[used],
                    send_sem=send_sums.at[used],
                    recv_sem=recv_sums.at[used],
                    device_id=device,
                    device_id_type=MESH,
                )
            )
            copies[-1].start()
            used += 1
        for copy in copies:
            copy.wait()
        total = sums[at]
        if at + 1 < len(phases):
            for n in range(len(phase)):
                total += sums_in[used - len(phase) + n]
            sums[at + 1] = total

    other = jnp.zeros_like(total)
    for n in range(len(phases[-1])):
        came = sums_in[used - len(phases[-1]) + n]
        place = lax.rem(ring + 2 * depth - (n + 1), 2 * depth)
        same = jnp.full(came.shape, place // depth, jnp.int32) == band
        total += jnp.where(same, came, 0.0)
        other += jnp.where(same, 0.0, came)
    own = total[:, :bands]
    mixed = total[:, bands : 2 * bands] + other[:, 2 * bands : 3 * bands]
    first = jnp.full(own.shape, band, jnp.int32) == 0
    weight = 1.0 / (tiles * ROWS * SZ)
    gram[:, :bands] = jnp.where(first, own, mixed) * weight
    gram[:, bands:] = jnp.where(first, mixed, own) * weight
    store.wait()


def per_device(tiles, psi, potential, projector, coupling, slot_live, point_count, point_index):
    bands = psi.shape[0]
    groups = bands // GB
    hbm = pl.BlockSpec(memory_space=pltpu.HBM)
    vmem = pl.BlockSpec(memory_space=pltpu.VMEM)
    filtered, gram = pl.pallas_call(
        functools.partial(kernel, tiles),
        out_shape=(
            jax.ShapeDtypeStruct((bands, ROWS, SZ), F32),
            jax.ShapeDtypeStruct((bands, 2 * bands), F32),
        ),
        in_specs=[hbm] * 7,
        out_specs=(hbm, vmem),
        scratch_shapes=[
            pltpu.VMEM((bands, ROWS, SZ), F32),
            pltpu.VMEM((bands, ROWS, SZ), F32),
            pltpu.VMEM((ROWS, SZ), F32),
            pltpu.VMEM((SLOTS, NPROJ, PTS), F32),
            pltpu.VMEM((NPROJ, SLOTS), F32),
            pltpu.SMEM((1,), jnp.int32),
            pltpu.SMEM((SLOTS,), jnp.int32),
            pltpu.VMEM((SLOTS, PTS), jnp.int32),
            pltpu.VMEM((2, groups, ROWS, GB, SZ), F32),
            pltpu.VMEM((2, groups, WIDTH * SY, GB, SZ), F32),
            pltpu.VMEM((2, groups, WIDTH * SY, GB, SZ), F32),
            pltpu.VMEM((2, groups, ROWS, GB, SZ), F32),
            pltpu.VMEM((groups, ROWS // 2, GB, SZ), F32),
            pltpu.VMEM((256, POINTS), BF16),
            pltpu.VMEM((16, POINTS), jnp.int32),
            pltpu.VMEM((16, POINTS), BF16),
            pltpu.VMEM((SLOTS, PTS, 2 * PTS), BF16),
            pltpu.VMEM((PAIRS, 16, 256), BF16),
            pltpu.VMEM((groups, PAIRS * 16, 256), F32),
            pltpu.VMEM((groups, ROWS, GB, SZ), F32),
            pltpu.VMEM((2 * bands, ROWS * SZ), BF16),
            pltpu.VMEM((2 * bands, ROWS * SZ // 2), BF16),
            pltpu.SemaphoreType.DMA((2, groups, 3)),
            pltpu.SemaphoreType.DMA((2, groups, 3)),
            pltpu.SemaphoreType.DMA((groups,)),
            pltpu.SemaphoreType.DMA((groups,)),
            pltpu.VMEM((4, bands, 128), F32),
            pltpu.VMEM((14, bands, 128), F32),
            pltpu.SemaphoreType.DMA((14,)),
            pltpu.SemaphoreType.DMA((14,)),
            pltpu.SemaphoreType.DMA((groups + 6,)),
        ],
        compiler_params=pltpu.CompilerParams(
            collective_id=0, has_side_effects=True, vmem_limit_bytes=62 << 20
        ),
        name="filter",
    )(
        psi.reshape(bands, ROWS, SZ),
        potential.reshape(ROWS, SZ),
        projector[0],
        jnp.swapaxes(coupling, 1, 2)[0],
        slot_live,
        point_count[0],
        point_index[0],
    )
    return filtered.reshape(psi.shape), gram


def solution(mesh):
    placed = (
        P("band", "space", None, None, None),
        P("space", None, None, None),
        P("space", None, None, None),
        P("space", None, None),
        P("space"),
        P("space", None),
        P("space", None, None),
    )
    return jax.shard_map(
        functools.partial(per_device, mesh.shape["space"]),
        mesh=mesh,
        in_specs=placed,
        out_specs=(P("band", "space", None, None, None), P("band", None)),
        check_vma=False,
    )
```

time: 717 us -> 81.3 us (0.11)
  blocking collectives: 337 us -> 0 us
  other arithmetic: 132 us -> 0 us
  local copies, waits for them, and re-layouts: 96.6 us -> 2.49 us
  Pallas kernels: 0 us -> 77.3 us
  waiting for transfers between devices: 73.5 us -> 0 us
  starting transfers between devices: 37 us -> 0 us
  matrix products: 18 us -> 0 us
  between operations: 15.4 us -> 1.29 us
    psum x1 -> x0, blocking collectives: 337 us -> none  [per_device(): rows_here = lax.psum(partial_rows, 'space')]
    scatter-add x4 -> x0, other arithmetic: 98.9 us -> none  [own_nonlocal(): jnp.zeros_like(flat).at[:, flat_index].add(contrib.reshape(band_rows, -1))]
    pallas_call x0 -> x1, Pallas kernels: none -> 77.3 us  [per_device(): pl.pallas_call(functools.partial(kernel, tiles), out_shape=(jax.ShapeDtyp...]
    gather x4 -> x0, local copies, waits for them, and re-layouts: 58.5 us -> none  [own_nonlocal(): values = jnp.take(flat, flat_index, axis=1).reshape(band_rows, slots, -1)]
    all_gather x1 -> x0, waiting for transfers between devices: 42 us -> none  [per_device(): lax.all_gather(flat_out, 'band', axis=0, tiled=True)]
    ppermute x12 -> x0, starting transfers between devices: 37 us -> none  [the longest x8 31.8 us: passed_along(): return lax.ppermute(block, axis, route)]
    ppermute x12 -> x0, waiting for transfers between devices: 31.5 us -> none  [the longest x8 31.5 us: passed_along(): return lax.ppermute(block, axis, route)]
    dot_general x9 -> x0, matrix products: 18 us -> none  [the longest x4 13.8 us: own_nonlocal(): jnp.einsum('sjp,bsp->bsj', weights, values, precision=lax.Precision.HIGHEST)]
  transfers between devices with their start and end apart: 13 -> 0, of which waited for: 4 -> 0; matrix products, arithmetic and copies ran while one was open for 23% -> 0% of each run, Pallas kernels for 0% -> 0%
where the time goes in v1:
time: 81.3 us; the launch traced here: 81.1 us
  Pallas kernels  77.3 us (95%)
  local copies, waits for them, and re-layouts  2.49 us (3%)
  between operations  1.29 us (2%)
    pallas_call x1, Pallas kernels, per_device(): pl.pallas_call(functools.partial(kernel, tiles), out_shape=(jax.ShapeDtyp...  77.3 us
    unnamed x4, local copies, waits for them, and re-layouts  2.49 us

profile of v1, /device:TPU:1, one launch (start us, length us, event | category | flops | bytes accessed | tf_op | source)
XLA Modules:
  0.0 81.1 jit_solution(8647709346410917529)
XLA Ops:
  1.3 77.3 %filter.1 = (f32[16,64,128]{2,1,0:T(8,128)}, f32[16,32]{1,0:T(8,128)}) custom-call(f32[16,64,128]{2,1,0:T(8,128)} %bitcast.11, f32[64,128]{1,0:T(8,128)} %bitcast.14, f32[32,16,128]{2,1,0:T(8,128)} %bitcast.13, f32[16,32]{1,0:T(8,128)} %bitcast.16, s32[1]{0:T(128)S(6)} %copy.12.slot_live_in, s32[32]{0:T(128)} %bitcast.17, s32[32,128]{1,0:T(8,128)} %bitcast.15), custom_call_target="tpu_custom_call" | custom-call | tf_op jit(solution)/shard_map/filter/pallas_call | solution.py:420
  78.5 0.0 copy-start
  78.6 1.9 %copy.13 = f32[16,1,8,8,128]{4,3,2,1,0:T(8,128)} copy(f32[16,1,8,8,128]{4,3,2,1,0:T(8,128)} %bitcast.12) | data formatting | bytes 1048576
  80.4 0.0 copy-done
  80.5 0.6 copy.14
Async XLA Ops:
  78.5 1.9 %copy-start = (f32[16,32]{1,0:T(8,128)S(1)}, f32[16,32]{1,0:T(8,128)}, u32[]{:S(2)}) copy-start(f32[16,32]{1,0:T(8,128)} %get-tuple-element.11) | copy-start | bytes 6148

commit v2 on v1

--- a/solution.py
+++ b/solution.py
@@ -25,11 +25,13 @@
 SX, SY, SZ = 8, 8, 128
 ROWS = SX * SY
 GB = 8
-PAIRS = ROWS // 2
+LOT = 4
+LOTS = ROWS // LOT
+PLACES = LOT * SZ
 SLOTS, NPROJ, PTS = 32, 16, 128
 POINTS = SLOTS * PTS
-CHUNK = 1024
-CHUNK_SLOTS = CHUNK // PTS
+CHUNK = 512
+PIECES = POINTS // CHUNK
 STEPS = 4
 
 
@@ -95,11 +97,12 @@
     other_y,
     other_band,
     hot,
-    pair_of,
-    pair_of16,
+    lot_of,
+    lot_of16,
     operator,
     parts,
     added,
+    given,
     local,
     wide,
     wide_other,
@@ -133,8 +136,7 @@
 
     phases = (
         [beside],
-        [turned_by(8, 2, away) for away in range(1, 4)],
-        [turned_by(32, 8, away) for away in range(1, 4)],
+        [turned_by(32, 2, away) for away in range(1, 16)],
         [along(away) for away in range(1, 2 * depth)],
     )
 
@@ -175,16 +177,24 @@
                 device_id_type=MESH,
             )
 
-        edge = WIDTH * SY
-        return (
-            copy(field.at[turn, g, pl.ds(ROWS - edge, edge)], low_x.at[turn, g], 0, up),
-            copy(field.at[turn, g, pl.ds(0, edge)], high_x.at[turn, g], 1, down),
-            copy(field.at[turn, g], other_y.at[turn, g], 2, beside),
-        )
+        block = field.at[turn, g]
+        copies = []
+        for half in range(2):
+            rows = pl.ds(half * LOT, LOT)
+            copies += [
+                copy(
+                    block.at[pl.ds(SX - WIDTH, WIDTH), rows],
+                    low_x.at[turn, g, :, rows],
+                    2 * half,
+                    up,
+                ),
+                copy(block.at[pl.ds(0, WIDTH), rows], high_x.at[turn, g, :, rows], 2 * half + 1, down),
+            ]
+        return copies + [copy(block, other_y.at[turn, g], 4, beside)]
 
     def band_copy(g):
         return pltpu.make_async_remote_copy(
-            src_ref=field.at[0, g, pl.ds(band * (ROWS // 2), ROWS // 2)],
+            src_ref=field.at[0, g, pl.ds(band * (SX // 2), SX // 2)],
             dst_ref=other_band.at[g],
             send_sem=send_band.at[g],
             recv_sem=recv_band.at[g],
@@ -192,14 +202,14 @@
             device_id_type=MESH,
         )
 
-    def split_pair(pair, first, second):
-        parts[pair] = two_parts(jnp.concatenate([first, second], axis=1))
+    def split_lot(g, lot, rows):
+        parts[g, lot] = two_parts(jnp.concatenate(rows, axis=1))
 
     for g in range(groups):
         loads[g].wait()
         for b in range(GB):
             for x in range(SX):
-                field[0, g, pl.ds(x * SY, SY), b, :] = psi[g * GB + b, pl.ds(x * SY, SY)]
+                field[0, g, x, :, b, :] = psi[g * GB + b, pl.ds(x * SY, SY)]
         if g == 0:
             pl.semaphore_wait(barrier, len(greeted))
         for copy in halo_copies(0, g):
@@ -209,16 +219,16 @@
     for copy in loads[groups:]:
         copy.wait()
 
-    @pl.loop(0, SLOTS, unroll=4)
+    @pl.loop(0, SLOTS, unroll=8)
     def _(s):
         cols = pl.ds(pl.multiple_of(s * PTS, PTS), PTS)
         index = point_index[pl.ds(s, 1), :]
-        place = jnp.broadcast_to(index & 255, (256, PTS))
-        spots = lax.broadcasted_iota(jnp.int32, (256, PTS), 0)
+        place = jnp.broadcast_to(index & (PLACES - 1), (PLACES, PTS))
+        spots = lax.broadcasted_iota(jnp.int32, (PLACES, PTS), 0)
         hot[:, cols] = jnp.where(place == spots, 1.0, 0.0).astype(BF16)
-        pair = jnp.broadcast_to(index >> 8, (16, PTS))
-        pair_of[:, cols] = pair
-        pair_of16[:, cols] = pair.astype(F32).astype(BF16)
+        lot = jnp.broadcast_to(index // PLACES, (16, PTS))
+        lot_of[:, cols] = lot
+        lot_of16[:, cols] = lot.astype(F32).astype(BF16)
         points = lax.broadcasted_iota(jnp.int32, (NPROJ, PTS), 1)
         slots = jnp.full((NPROJ, PTS), s, jnp.int32)
         keep = (points < point_count[s]) & (slots < slot_live[0])
@@ -234,34 +244,51 @@
         square_high = square.astype(BF16).astype(F32)
         operator[s] = jnp.concatenate([square_high, square - square_high], axis=1).astype(BF16)
 
-    def nonlocal_chunk(g, c):
-        cols = pl.ds(c * CHUNK, CHUNK)
-        one_hot = hot[:, cols]
-        picked = dot(parts[...].reshape(PAIRS * 16, 256), one_hot)
-        pairs = pair_of[:, cols]
+    def gathered(g, piece):
+        cols = pl.ds(piece * CHUNK, CHUNK)
+        picked = dot(parts[g].reshape(LOTS * 16, PLACES), hot[:, cols])
+        lots = lot_of[:, cols]
         values = jnp.zeros((16, CHUNK), F32)
-        for pair in range(PAIRS):
-            values = jnp.where(pairs == pair, picked[16 * pair : 16 * pair + 16], values)
-        values = values[:8] + values[8:]
+        for lot in range(LOTS):
+            values = jnp.where(lots == lot, picked[16 * lot : 16 * lot + 16], values)
+        return values[:8] + values[8:]
+
+    def operated(values, piece):
         given = []
-        for s in range(CHUNK_SLOTS):
-            product = dot(two_parts(values[:, s * PTS : (s + 1) * PTS]), operator[c * CHUNK_SLOTS + s])
-            given.append(
-                two_parts(product[:8, :PTS] + (product[:8, PTS:] + product[8:, :PTS]))
+        nothing = jnp.zeros((16, PTS), BF16)
+        for s in range(0, CHUNK // PTS, 2):
+            first = two_parts(values[:, s * PTS : (s + 1) * PTS])
+            second = two_parts(values[:, (s + 1) * PTS : (s + 2) * PTS])
+            both = jnp.concatenate(
+                [
+                    jnp.concatenate([first, nothing], axis=1),
+                    jnp.concatenate([nothing, second], axis=1),
+                ],
+                axis=0,
             )
-        given = jnp.concatenate(given, axis=1)
-        pairs = pair_of16[:, cols]
-        nothing = jnp.zeros_like(given)
-        spread = [jnp.where(pairs == pair, given, nothing) for pair in range(PAIRS)]
-        term = dot_t(jnp.concatenate(spread, axis=0), one_hot)
-        if c == 0:
-            added[g] = term
-        else:
-            added[g] += term
+            at = piece * (CHUNK // PTS) + s
+            products = dot(both, operator[at : at + 2].reshape(2 * PTS, 2 * PTS))
+            for product in (products[:16], products[16:]):
+                given.append(
+                    two_parts(product[:8, :PTS] + (product[:8, PTS:] + product[8:, :PTS]))
+                )
+        return jnp.concatenate(given, axis=1)
+
+    def gather_and_operate(g):
+        values = [gathered(g, piece) for piece in range(PIECES)]
+        for piece in range(PIECES):
+            given[:, piece * CHUNK : (piece + 1) * CHUNK] = operated(values[piece], piece)
+
+    def scatter():
+        amounts = given[...]
+        lots = lot_of16[...]
+        nothing = jnp.zeros_like(amounts)
+        spread = [jnp.where(lots == lot, amounts, nothing) for lot in range(LOTS)]
+        added[...] = dot_t(jnp.concatenate(spread, axis=0), hot[...])
 
     def stencil_plane(turn, g, x, diagonal):
-        own = [field[turn, g, x * SY + y] for y in range(SY)]
-        ring = own + [other_y[turn, g, x * SY + y] for y in range(SY)]
+        own = [field[turn, g, x, y] for y in range(SY)]
+        ring = own + [other_y[turn, g, x, y] for y in range(SY)]
         for y in range(SY):
             value = own[y]
             total = value * (jnp.broadcast_to(pot[pl.ds(x * SY + y, 1)], (GB, SZ)) + diagonal)
@@ -269,108 +296,119 @@
                 near = ring[(y + k) % (2 * SY)] + ring[(y - k) % (2 * SY)]
                 near += pltpu.roll(value, k, axis=1) + pltpu.roll(value, SZ - k, axis=1)
                 if x - k >= 0:
-                    near += field[turn, g, (x - k) * SY + y]
+                    near += field[turn, g, x - k, y]
                 if x + k < SX:
-                    near += field[turn, g, (x + k) * SY + y]
+                    near += field[turn, g, x + k, y]
                 total += (KINETIC * LAP_COEFFS[k]) * near
-            local[g, x * SY + y] = total
-
-    def apply_local(step, turn, g):
-        diagonal = 3.0 * KINETIC * LAP_COEFFS[0] - chosen(step, SHIFT)
-        nonlocal_chunk(g, 0)
-        nonlocal_chunk(g, 1)
-        halo_copies(turn, g)[2].wait_recv()
-        nonlocal_chunk(g, 2)
-        for x in range(4):
-            stencil_plane(turn, g, x, diagonal)
-        nonlocal_chunk(g, 3)
-        for x in range(4, 8):
-            stencil_plane(turn, g, x, diagonal)
-
-    def finish(step, turn, g):
+            local[g, x, y] = total
+
+    def finish(step, turn, g, half):
+        for copy in halo_copies(turn, g)[2 * half : 2 * half + 2]:
+            copy.wait()
         scale, carry = chosen(step, SCALE), chosen(step, CARRY)
-        for y in range(0, SY, 2):
-            lower = [[low_x[turn, g, j * SY + y + e] for j in range(WIDTH)] for e in range(2)]
-            upper = [[high_x[turn, g, j * SY + y + e] for j in range(WIDTH)] for e in range(2)]
-            for x in range(SX):
-                pair = x * (SY // 2) + y // 2
-                spread = added[g, pl.ds(16 * pair, 16)]
-                spread = spread[:8] + spread[8:]
-                new = []
-                for e in range(2):
-                    row = x * SY + y + e
-                    total = local[g, row] + spread[:, e * SZ : (e + 1) * SZ]
-                    for j in range(WIDTH):
-                        if j >= x:
-                            total += (KINETIC * LAP_COEFFS[x + WIDTH - j]) * lower[e][j]
-                        if j <= x - 2:
-                            total += (KINETIC * LAP_COEFFS[SX + j - x]) * upper[e][j]
-                    value = scale * total + carry * field[1 - turn, g, row]
-                    field[1 - turn, g, row] = value
-                    new.append(value)
-                split_pair(pair, new[0], new[1])
-
-    for g in range(groups):
-        for pair in range(PAIRS):
-            split_pair(pair, field[0, g, 2 * pair], field[0, g, 2 * pair + 1])
-        apply_local(0, 0, g)
-
-    @pl.loop(0, STEPS * groups)
-    def _(at):
-        step = at // groups
-        g = lax.rem(at, groups)
-        turn = lax.rem(step, 2)
-        copies = halo_copies(turn, g)
-        copies[0].wait()
-        copies[1].wait()
-        copies[2].wait_send()
-        finish(step, turn, g)
+        for x in range(SX):
+            lot = x * (SY // LOT) + half
+            spread = added[pl.ds(16 * lot, 16)]
+            spread = spread[:8] + spread[8:]
+            new = []
+            for e in range(LOT):
+                y = half * LOT + e
+                total = local[g, x, y] + spread[:, e * SZ : (e + 1) * SZ]
+                for j in range(WIDTH):
+                    if j >= x:
+                        total += (KINETIC * LAP_COEFFS[x + WIDTH - j]) * low_x[turn, g, j, y]
+                    if j <= x - 2:
+                        total += (KINETIC * LAP_COEFFS[SX + j - x]) * high_x[turn, g, j, y]
+                value = scale * total + carry * field[1 - turn, g, x, y]
+                field[1 - turn, g, x, y] = value
+                new.append(value)
+            split_lot(g, lot, new)
 
         @pl.when(step < STEPS - 1)
         def _():
-            for copy in halo_copies(1 - turn, g):
+            following = halo_copies(1 - turn, g)
+            for copy in following[2 * half : 2 * half + 2] + following[4:] * half:
                 copy.start()
-            apply_local(step + 1, 1 - turn, g)
-
-        @pl.when(step == STEPS - 1)
+
+        if half == 1:
+
+            @pl.when(step == STEPS - 1)
+            def _():
+                band_copy(g).start()
+
+    for g in range(groups):
+        for lot in range(LOTS):
+            x, half = lot // (SY // LOT), lot % (SY // LOT)
+            split_lot(g, lot, [field[0, g, x, half * LOT + e] for e in range(LOT)])
+
+    rounds = STEPS * groups
+
+    def place_of(at):
+        step = at // groups
+        return step, step % 2, at % groups
+
+    @pl.loop(0, rounds)
+    def _(at):
+        step, turn, g = place_of(at)
+        diagonal = 3.0 * KINETIC * LAP_COEFFS[0] - chosen(step, SHIFT)
+        halo_copies(turn, g)[4].wait()
+        gather_and_operate(g)
+        for x in range(SX // 2):
+            stencil_plane(turn, g, x, diagonal)
+
+        @pl.when(at > 0)
         def _():
-            band_copy(g).start()
+            finish(*place_of(lax.rem(at + rounds - 1, rounds)), 1)
+
+        scatter()
+        for x in range(SX // 2, SX):
+            stencil_plane(turn, g, x, diagonal)
+        finish(step, turn, g, 0)
+
+    finish(*place_of(rounds - 1), 1)
 
     bands = groups * GB
     for g in range(groups):
         for b in range(GB):
             for x in range(SX):
-                ready[g * GB + b, pl.ds(x * SY, SY)] = field[0, g, pl.ds(x * SY, SY), b, :]
+                ready[g * GB + b, pl.ds(x * SY, SY)] = field[0, g, x, :, b, :]
     store = loaded(ready, out, groups)
     store.start()
 
     @pl.loop(0, ROWS, unroll=8)
     def _(row):
         cols = pl.ds(pl.multiple_of(row * SZ, SZ), SZ)
-        wide[:, cols] = two_parts(jnp.concatenate([field[0, g, row] for g in range(groups)], axis=0))
+        wide[:, cols] = two_parts(jnp.concatenate([field[0, g, row // SY, row % SY] for g in range(groups)], axis=0))
 
     def folded(product):
-        return (product[:bands, :bands] + product[bands:, bands:]) + (
-            product[:bands, bands:] + product[bands:, :bands]
+        rows, cols = product.shape[0] // 2, product.shape[1] // 2
+        return (product[:rows, :cols] + product[rows:, cols:]) + (
+            product[:rows, cols:] + product[rows:, :cols]
         )
 
+    def keep_term(term, row, col):
+        for at in range(0, term.shape[0], GB):
+            lane = (row + at) // GB * 64 + col
+            sums[0, :, lane : lane + term.shape[1]] = term[at : at + GB]
+
+    def kept_term(sum_, col):
+        return jnp.concatenate([sum_[:, col : col + bands], sum_[:, 64 + col : 64 + col + bands]], axis=0)
+
+    sums[0] = jnp.zeros(sums.shape[1:], F32)
     block = wide[...]
-    sums[0, :, :bands] = folded(dot_t(block, block))
+    keep_term(folded(dot_t(block, block)), 0, 0)
+
+    half = ROWS // 2 * SZ
+    kept = wide[:, pl.ds(pl.multiple_of((1 - band) * half, half), half)]
     for g in range(groups):
         band_copy(g).wait()
-
-    @pl.loop(0, ROWS // 2, unroll=8)
-    def _(row):
-        cols = pl.ds(pl.multiple_of(row * SZ, SZ), SZ)
-        wide_other[:, cols] = two_parts(
-            jnp.concatenate([other_band[g, row] for g in range(groups)], axis=0)
-        )
-
-    half = ROWS // 2 * SZ
-    kept = wide[:, pl.ds(pl.multiple_of((1 - band) * half, half), half)]
-    came = wide_other[...]
-    sums[0, :, bands : 2 * bands] = folded(dot_t(kept, came))
-    sums[0, :, 2 * bands : 3 * bands] = folded(dot_t(came, kept))
+        for row in range(ROWS // 2):
+            wide_other[g, :, row * SZ : (row + 1) * SZ] = two_parts(
+                other_band[g, row // SY, row % SY]
+            )
+        came = wide_other[g]
+        keep_term(folded(dot_t(kept, came)), 0, bands + g * GB)
+        keep_term(folded(dot_t(came, kept)), g * GB, 2 * bands)
 
     used = 0
     for at, phase in enumerate(phases):
@@ -403,8 +441,8 @@
         same = jnp.full(came.shape, place // depth, jnp.int32) == band
         total += jnp.where(same, came, 0.0)
         other += jnp.where(same, 0.0, came)
-    own = total[:, :bands]
-    mixed = total[:, bands : 2 * bands] + other[:, 2 * bands : 3 * bands]
+    own = kept_term(total, 0)
+    mixed = kept_term(total, bands) + kept_term(other, 2 * bands)
     first = jnp.full(own.shape, band, jnp.int32) == 0
     weight = 1.0 / (tiles * ROWS * SZ)
     gram[:, :bands] = jnp.where(first, own, mixed) * weight
@@ -434,28 +472,29 @@
             pltpu.SMEM((1,), jnp.int32),
             pltpu.SMEM((SLOTS,), jnp.int32),
             pltpu.VMEM((SLOTS, PTS), jnp.int32),
-            pltpu.VMEM((2, groups, ROWS, GB, SZ), F32),
-            pltpu.VMEM((2, groups, WIDTH * SY, GB, SZ), F32),
-            pltpu.VMEM((2, groups, WIDTH * SY, GB, SZ), F32),
-            pltpu.VMEM((2, groups, ROWS, GB, SZ), F32),
-            pltpu.VMEM((groups, ROWS // 2, GB, SZ), F32),
-            pltpu.VMEM((256, POINTS), BF16),
+            pltpu.VMEM((2, groups, SX, SY, GB, SZ), F32),
+            pltpu.VMEM((2, groups, WIDTH, SY, GB, SZ), F32),
+            pltpu.VMEM((2, groups, WIDTH, SY, GB, SZ), F32),
+            pltpu.VMEM((2, groups, SX, SY, GB, SZ), F32),
+            pltpu.VMEM((groups, SX // 2, SY, GB, SZ), F32),
+            pltpu.VMEM((PLACES, POINTS), BF16),
             pltpu.VMEM((16, POINTS), jnp.int32),
             pltpu.VMEM((16, POINTS), BF16),
             pltpu.VMEM((SLOTS, PTS, 2 * PTS), BF16),
-            pltpu.VMEM((PAIRS, 16, 256), BF16),
-            pltpu.VMEM((groups, PAIRS * 16, 256), F32),
-            pltpu.VMEM((groups, ROWS, GB, SZ), F32),
+            pltpu.VMEM((groups, LOTS, 16, PLACES), BF16),
+            pltpu.VMEM((LOTS * 16, PLACES), F32),
+            pltpu.VMEM((16, POINTS), BF16),
+            pltpu.VMEM((groups, SX, SY, GB, SZ), F32),
             pltpu.VMEM((2 * bands, ROWS * SZ), BF16),
-            pltpu.VMEM((2 * bands, ROWS * SZ // 2), BF16),
-            pltpu.SemaphoreType.DMA((2, groups, 3)),
-            pltpu.SemaphoreType.DMA((2, groups, 3)),
+            pltpu.VMEM((groups, 2 * GB, ROWS * SZ // 2), BF16),
+            pltpu.SemaphoreType.DMA((2, groups, 5)),
+            pltpu.SemaphoreType.DMA((2, groups, 5)),
             pltpu.SemaphoreType.DMA((groups,)),
             pltpu.SemaphoreType.DMA((groups,)),
-            pltpu.VMEM((4, bands, 128), F32),
-            pltpu.VMEM((14, bands, 128), F32),
-            pltpu.SemaphoreType.DMA((14,)),
-            pltpu.SemaphoreType.DMA((14,)),
+            pltpu.VMEM((3, GB, 128), F32),
+            pltpu.VMEM((23, GB, 128), F32),
+            pltpu.SemaphoreType.DMA((23,)),
+            pltpu.SemaphoreType.DMA((23,)),
             pltpu.SemaphoreType.DMA((groups + 6,)),
         ],
         compiler_params=pltpu.CompilerParams(

time: 81.3 us -> 74.4 us (0.915)
  Pallas kernels: 77.3 us -> 70.5 us
    pallas_call x1, Pallas kernels: 77.3 us -> 70.5 us  [per_device(): pl.pallas_call(functools.partial(kernel, tiles), out_shape=(jax.ShapeDtyp...]
where the time goes in v2:
time: 74.4 us; the launch traced here: 74.3 us
  Pallas kernels  70.5 us (95%)
  local copies, waits for them, and re-layouts  2.49 us (3%)
  between operations  1.29 us (2%)
    pallas_call x1, Pallas kernels, per_device(): pl.pallas_call(functools.partial(kernel, tiles), out_shape=(jax.ShapeDtyp...  70.5 us
    unnamed x4, local copies, waits for them, and re-layouts  2.49 us

profile of v2, /device:TPU:1, one launch (start us, length us, event | category | flops | bytes accessed | tf_op | source)
XLA Modules:
  0.0 74.3 jit_solution(16857190928132185754)
XLA Ops:
  1.3 70.5 %filter.1 = (f32[16,64,128]{2,1,0:T(8,128)}, f32[16,32]{1,0:T(8,128)}) custom-call(f32[16,64,128]{2,1,0:T(8,128)} %bitcast.11, f32[64,128]{1,0:T(8,128)} %bitcast.14, f32[32,16,128]{2,1,0:T(8,128)} %bitcast.13, f32[16,32]{1,0:T(8,128)} %bitcast.16, s32[1]{0:T(128)S(6)} %copy.12.slot_live_in, s32[32]{0:T(128)} %bitcast.17, s32[32,128]{1,0:T(8,128)} %bitcast.15), custom_call_target="tpu_custom_call" | custom-call | tf_op jit(solution)/shard_map/filter/pallas_call | solution.py:458
  71.8 0.0 copy-start
  71.8 1.9 %copy.13 = f32[16,1,8,8,128]{4,3,2,1,0:T(8,128)} copy(f32[16,1,8,8,128]{4,3,2,1,0:T(8,128)} %bitcast.12) | data formatting | bytes 1048576
  73.7 0.0 copy-done
  73.7 0.6 copy.14
Async XLA Ops:
  71.8 1.9 %copy-start = (f32[16,32]{1,0:T(8,128)S(1)}, f32[16,32]{1,0:T(8,128)}, u32[]{:S(2)}) copy-start(f32[16,32]{1,0:T(8,128)} %get-tuple-element.11) | copy-start | bytes 6148

commit v3 on v2

--- a/solution.py
+++ b/solution.py
@@ -32,6 +32,7 @@
 POINTS = SLOTS * PTS
 CHUNK = 512
 PIECES = POINTS // CHUNK
+LANE_PIECES = (3, 5, 7)
 STEPS = 4
 
 
@@ -78,17 +79,15 @@
     pot_in,
     projector_in,
     coupling_in,
-    slot_live_in,
+    slot_live,
     point_count_in,
     point_index_in,
     out,
     gram,
-    ready,
     psi,
     pot,
     projector,
     coupling,
-    slot_live,
     point_count,
     point_index,
     field,
@@ -99,6 +98,8 @@
     hot,
     lot_of,
     lot_of16,
+    row_of,
+    lane_of,
     operator,
     parts,
     added,
@@ -157,7 +158,6 @@
                 (point_index_in, point_index),
                 (projector_in, projector),
                 (coupling_in, coupling),
-                (slot_live_in, slot_live),
                 (point_count_in, point_count),
                 (pot_in, pot),
             )
@@ -192,12 +192,13 @@
             ]
         return copies + [copy(block, other_y.at[turn, g], 4, beside)]
 
-    def band_copy(g):
+    def band_copy(g, half):
+        rows = pl.ds(half * LOT, LOT)
         return pltpu.make_async_remote_copy(
-            src_ref=field.at[0, g, pl.ds(band * (SX // 2), SX // 2)],
-            dst_ref=other_band.at[g],
-            send_sem=send_band.at[g],
-            recv_sem=recv_band.at[g],
+            src_ref=field.at[0, g, pl.ds(band * (SX // 2), SX // 2), rows],
+            dst_ref=other_band.at[g, :, rows],
+            send_sem=send_band.at[g, half],
+            recv_sem=recv_band.at[g, half],
             device_id=across,
             device_id_type=MESH,
         )
@@ -226,6 +227,8 @@
         place = jnp.broadcast_to(index & (PLACES - 1), (PLACES, PTS))
         spots = lax.broadcasted_iota(jnp.int32, (PLACES, PTS), 0)
         hot[:, cols] = jnp.where(place == spots, 1.0, 0.0).astype(BF16)
+        row_of[:, cols] = jnp.broadcast_to(index // SZ, (GB, PTS))
+        lane_of[:, cols] = jnp.broadcast_to(index & (SZ - 1), (GB, PTS))
         lot = jnp.broadcast_to(index // PLACES, (16, PTS))
         lot_of[:, cols] = lot
         lot_of16[:, cols] = lot.astype(F32).astype(BF16)
@@ -252,6 +255,20 @@
         for lot in range(LOTS):
             values = jnp.where(lots == lot, picked[16 * lot : 16 * lot + 16], values)
         return values[:8] + values[8:]
+
+    def gathered_by_lanes(turn, g, piece):
+        values = []
+        for s in range(CHUNK // PTS):
+            cols = pl.ds(piece * CHUNK + s * PTS, PTS)
+            lanes, rows = lane_of[:, cols], row_of[:, cols]
+            found = jnp.zeros((GB, PTS), F32)
+            for row in range(ROWS):
+                picked = jnp.take_along_axis(
+                    field[turn, g, row // SY, row % SY], lanes, axis=1, mode="promise_in_bounds"
+                )
+                found = jnp.where(rows == row, picked, found)
+            values.append(found)
+        return jnp.concatenate(values, axis=1)
 
     def operated(values, piece):
         given = []
@@ -274,8 +291,11 @@
                 )
         return jnp.concatenate(given, axis=1)
 
-    def gather_and_operate(g):
-        values = [gathered(g, piece) for piece in range(PIECES)]
+    def gather_and_operate(turn, g):
+        values = [
+            gathered_by_lanes(turn, g, piece) if piece in LANE_PIECES else gathered(g, piece)
+            for piece in range(PIECES)
+        ]
         for piece in range(PIECES):
             given[:, piece * CHUNK : (piece + 1) * CHUNK] = operated(values[piece], piece)
 
@@ -330,11 +350,9 @@
             for copy in following[2 * half : 2 * half + 2] + following[4:] * half:
                 copy.start()
 
-        if half == 1:
-
-            @pl.when(step == STEPS - 1)
-            def _():
-                band_copy(g).start()
+        @pl.when(step == STEPS - 1)
+        def _():
+            band_copy(g, half).start()
 
     for g in range(groups):
         for lot in range(LOTS):
@@ -352,7 +370,7 @@
         step, turn, g = place_of(at)
         diagonal = 3.0 * KINETIC * LAP_COEFFS[0] - chosen(step, SHIFT)
         halo_copies(turn, g)[4].wait()
-        gather_and_operate(g)
+        gather_and_operate(turn, g)
         for x in range(SX // 2):
             stencil_plane(turn, g, x, diagonal)
 
@@ -371,14 +389,19 @@
     for g in range(groups):
         for b in range(GB):
             for x in range(SX):
-                ready[g * GB + b, pl.ds(x * SY, SY)] = field[0, g, x, :, b, :]
-    store = loaded(ready, out, groups)
-    store.start()
-
-    @pl.loop(0, ROWS, unroll=8)
-    def _(row):
-        cols = pl.ds(pl.multiple_of(row * SZ, SZ), SZ)
-        wide[:, cols] = two_parts(jnp.concatenate([field[0, g, row // SY, row % SY] for g in range(groups)], axis=0))
+                out[g * GB + b, pl.ds(x * SY, SY)] = field[0, g, x, :, b, :]
+    quarter = ROWS // 4
+
+    def quarter_rows():
+        return [(x, y) for x in range(SX // 2) for y in range(LOT)]
+
+    for at in range(4):
+        for n, (x, y) in enumerate(quarter_rows()):
+            x, y = x + at // 2 * (SX // 2), y + at % 2 * LOT
+            row = at * quarter + n
+            wide[:, row * SZ : (row + 1) * SZ] = two_parts(
+                jnp.concatenate([field[0, g, x, y] for g in range(groups)], axis=0)
+            )
 
     def folded(product):
         rows, cols = product.shape[0] // 2, product.shape[1] // 2
@@ -398,17 +421,20 @@
     block = wide[...]
     keep_term(folded(dot_t(block, block)), 0, 0)
 
-    half = ROWS // 2 * SZ
-    kept = wide[:, pl.ds(pl.multiple_of((1 - band) * half, half), half)]
+    depth_of = quarter * SZ
     for g in range(groups):
-        band_copy(g).wait()
-        for row in range(ROWS // 2):
-            wide_other[g, :, row * SZ : (row + 1) * SZ] = two_parts(
-                other_band[g, row // SY, row % SY]
-            )
-        came = wide_other[g]
-        keep_term(folded(dot_t(kept, came)), 0, bands + g * GB)
-        keep_term(folded(dot_t(came, kept)), g * GB, 2 * bands)
+        term = None
+        for half in range(2):
+            start = (2 * (1 - band) + half) * depth_of
+            kept = wide[:, pl.ds(pl.multiple_of(start, depth_of), depth_of)]
+            band_copy(g, half).wait()
+            for n, (x, y) in enumerate(quarter_rows()):
+                wide_other[:, n * SZ : (n + 1) * SZ] = two_parts(
+                    other_band[g, x, half * LOT + y]
+                )
+            part = dot_t(kept, wide_other[...])
+            term = part if term is None else term + part
+        keep_term(folded(term), 0, bands + g * GB)
 
     used = 0
     for at, phase in enumerate(phases):
@@ -442,12 +468,15 @@
         total += jnp.where(same, came, 0.0)
         other += jnp.where(same, 0.0, came)
     own = kept_term(total, 0)
-    mixed = kept_term(total, bands) + kept_term(other, 2 * bands)
+    mixed = kept_term(total, bands) + kept_term(other, bands).T
     first = jnp.full(own.shape, band, jnp.int32) == 0
     weight = 1.0 / (tiles * ROWS * SZ)
     gram[:, :bands] = jnp.where(first, own, mixed) * weight
     gram[:, bands:] = jnp.where(first, mixed, own) * weight
-    store.wait()
+
+
+def in_hbm(array):
+    return pltpu.with_memory_space_constraint(array, pltpu.HBM)
 
 
 def per_device(tiles, psi, potential, projector, coupling, slot_live, point_count, point_index):
@@ -455,21 +484,20 @@
     groups = bands // GB
     hbm = pl.BlockSpec(memory_space=pltpu.HBM)
     vmem = pl.BlockSpec(memory_space=pltpu.VMEM)
+    smem = pl.BlockSpec(memory_space=pltpu.SMEM)
     filtered, gram = pl.pallas_call(
         functools.partial(kernel, tiles),
         out_shape=(
             jax.ShapeDtypeStruct((bands, ROWS, SZ), F32),
             jax.ShapeDtypeStruct((bands, 2 * bands), F32),
         ),
-        in_specs=[hbm] * 7,
-        out_specs=(hbm, vmem),
+        in_specs=[hbm] * 4 + [smem] + [hbm] * 2,
+        out_specs=(vmem, vmem),
         scratch_shapes=[
-            pltpu.VMEM((bands, ROWS, SZ), F32),
             pltpu.VMEM((bands, ROWS, SZ), F32),
             pltpu.VMEM((ROWS, SZ), F32),
             pltpu.VMEM((SLOTS, NPROJ, PTS), F32),
             pltpu.VMEM((NPROJ, SLOTS), F32),
-            pltpu.SMEM((1,), jnp.int32),
             pltpu.SMEM((SLOTS,), jnp.int32),
             pltpu.VMEM((SLOTS, PTS), jnp.int32),
             pltpu.VMEM((2, groups, SX, SY, GB, SZ), F32),
@@ -480,17 +508,19 @@
             pltpu.VMEM((PLACES, POINTS), BF16),
             pltpu.VMEM((16, POINTS), jnp.int32),
             pltpu.VMEM((16, POINTS), BF16),
+            pltpu.VMEM((GB, POINTS), jnp.int32),
+            pltpu.VMEM((GB, POINTS), jnp.int32),
             pltpu.VMEM((SLOTS, PTS, 2 * PTS), BF16),
             pltpu.VMEM((groups, LOTS, 16, PLACES), BF16),
             pltpu.VMEM((LOTS * 16, PLACES), F32),
             pltpu.VMEM((16, POINTS), BF16),
             pltpu.VMEM((groups, SX, SY, GB, SZ), F32),
             pltpu.VMEM((2 * bands, ROWS * SZ), BF16),
-            pltpu.VMEM((groups, 2 * GB, ROWS * SZ // 2), BF16),
+            pltpu.VMEM((2 * GB, ROWS * SZ // 4), BF16),
             pltpu.SemaphoreType.DMA((2, groups, 5)),
             pltpu.SemaphoreType.DMA((2, groups, 5)),
-            pltpu.SemaphoreType.DMA((groups,)),
-            pltpu.SemaphoreType.DMA((groups,)),
+            pltpu.SemaphoreType.DMA((groups, 2)),
+            pltpu.SemaphoreType.DMA((groups, 2)),
             pltpu.VMEM((3, GB, 128), F32),
             pltpu.VMEM((23, GB, 128), F32),
             pltpu.SemaphoreType.DMA((23,)),
@@ -498,17 +528,17 @@
             pltpu.SemaphoreType.DMA((groups + 6,)),
         ],
         compiler_params=pltpu.CompilerParams(
-            collective_id=0, has_side_effects=True, vmem_limit_bytes=62 << 20
+            collective_id=0, has_side_effects=True, vmem_limit_bytes=40 << 20
         ),
         name="filter",
     )(
-        psi.reshape(bands, ROWS, SZ),
-        potential.reshape(ROWS, SZ),
-        projector[0],
-        jnp.swapaxes(coupling, 1, 2)[0],
+        in_hbm(psi.reshape(bands, ROWS, SZ)),
+        in_hbm(potential.reshape(ROWS, SZ)),
+        in_hbm(projector[0]),
+        in_hbm(jnp.swapaxes(coupling, 1, 2)[0]),
         slot_live,
-        point_count[0],
-        point_index[0],
+        in_hbm(point_count[0]),
+        in_hbm(point_index[0]),
     )
     return filtered.reshape(psi.shape), gram
 

time: 74.4 us -> 72.9 us (0.980)
  local copies, waits for them, and re-layouts: 2.49 us -> 1.39 us
    unnamed x4 -> x2, local copies, waits for them, and re-layouts: 2.49 us -> 1.39 us
where the time goes in v3:
time: 72.9 us; the launch traced here: 72.8 us
  Pallas kernels  70.1 us (96%)
  local copies, waits for them, and re-layouts  1.39 us (2%)
  between operations  1.29 us (2%)
    pallas_call x1, Pallas kernels, per_device(): pl.pallas_call(functools.partial(kernel, tiles), out_shape=(jax.ShapeDtyp...  70.1 us

profile of v3, /device:TPU:1, one launch (start us, length us, event | category | flops | bytes accessed | tf_op | source)
XLA Modules:
  0.0 72.8 jit_solution(13454164007964285806)
XLA Ops:
  1.3 70.1 %filter.1 = (f32[16,64,128]{2,1,0:T(8,128)S(1)}, f32[16,32]{1,0:T(8,128)S(1)}) custom-call(f32[16,64,128]{2,1,0:T(8,128)} %bitcast.12, f32[64,128]{1,0:T(8,128)} %bitcast.14, f32[32,16,128]{2,1,0:T(8,128)} %bitcast.13, f32[16,32]{1,0:T(8,128)} %bitcast.16, s32[1]{0:T(128)S(6)} %copy.12.slot_live, s32[32]{0:T(128)} %bitcast.17, s32[32,128]{1,0:T(8,128)} %bitcast.15), custom_call_target="tpu_custom_call" | custom-call | tf_op jit(solution)/shard_map/filter/pallas_call | solution.py:488
  71.4 0.8 %copy.13 = f32[16,1,8,8,128]{4,3,2,1,0:T(8,128)} copy(f32[16,1,8,8,128]{4,3,2,1,0:T(8,128)S(1)} %bitcast.11) | data formatting | bytes 1048576
  72.2 0.6 copy.14

commit v4 on v3

--- a/solution.py
+++ b/solution.py
@@ -141,11 +141,6 @@
         [along(away) for away in range(1, 2 * depth)],
     )
 
-    barrier = pltpu.get_barrier_semaphore()
-    greeted = [up, down] + [device for phase in phases for device in phase]
-    for device in greeted:
-        pl.semaphore_signal(barrier, inc=1, device_id=device, device_id_type=MESH)
-
     def loaded(src, dst, at):
         return pltpu.make_async_copy(src, dst, load.at[at])
 
@@ -163,7 +158,14 @@
             )
         )
     ]
-    for copy in loads:
+    for copy in loads[:groups]:
+        copy.start()
+
+    greeted = [device for phase in phases[::-1] for device in phase] + [up, down]
+    barrier = pltpu.get_barrier_semaphore()
+    for device in greeted:
+        pl.semaphore_signal(barrier, inc=1, device_id=device, device_id_type=MESH)
+    for copy in loads[groups:]:
         copy.start()
 
     def halo_copies(turn, g):
@@ -299,12 +301,12 @@
         for piece in range(PIECES):
             given[:, piece * CHUNK : (piece + 1) * CHUNK] = operated(values[piece], piece)
 
-    def scatter():
+    def scatter(g):
         amounts = given[...]
         lots = lot_of16[...]
         nothing = jnp.zeros_like(amounts)
         spread = [jnp.where(lots == lot, amounts, nothing) for lot in range(LOTS)]
-        added[...] = dot_t(jnp.concatenate(spread, axis=0), hot[...])
+        added[g] = dot_t(jnp.concatenate(spread, axis=0), hot[...])
 
     def stencil_plane(turn, g, x, diagonal):
         own = [field[turn, g, x, y] for y in range(SY)]
@@ -328,7 +330,7 @@
         scale, carry = chosen(step, SCALE), chosen(step, CARRY)
         for x in range(SX):
             lot = x * (SY // LOT) + half
-            spread = added[pl.ds(16 * lot, 16)]
+            spread = added[g, pl.ds(16 * lot, 16)]
             spread = spread[:8] + spread[8:]
             new = []
             for e in range(LOT):
@@ -368,21 +370,24 @@
     @pl.loop(0, rounds)
     def _(at):
         step, turn, g = place_of(at)
-        diagonal = 3.0 * KINETIC * LAP_COEFFS[0] - chosen(step, SHIFT)
-        halo_copies(turn, g)[4].wait()
+        before = place_of(lax.rem(at + rounds - 1, rounds))
         gather_and_operate(turn, g)
-        for x in range(SX // 2):
-            stencil_plane(turn, g, x, diagonal)
 
         @pl.when(at > 0)
         def _():
-            finish(*place_of(lax.rem(at + rounds - 1, rounds)), 1)
-
-        scatter()
-        for x in range(SX // 2, SX):
+            finish(*before, 0)
+
+        halo_copies(turn, g)[4].wait()
+        scatter(g)
+        diagonal = 3.0 * KINETIC * LAP_COEFFS[0] - chosen(step, SHIFT)
+        for x in range(SX):
             stencil_plane(turn, g, x, diagonal)
-        finish(step, turn, g, 0)
-
+
+        @pl.when(at > 0)
+        def _():
+            finish(*before, 1)
+
+    finish(*place_of(rounds - 1), 0)
     finish(*place_of(rounds - 1), 1)
 
     bands = groups * GB
@@ -512,7 +517,7 @@
             pltpu.VMEM((GB, POINTS), jnp.int32),
             pltpu.VMEM((SLOTS, PTS, 2 * PTS), BF16),
             pltpu.VMEM((groups, LOTS, 16, PLACES), BF16),
-            pltpu.VMEM((LOTS * 16, PLACES), F32),
+            pltpu.VMEM((groups, LOTS * 16, PLACES), F32),
             pltpu.VMEM((16, POINTS), BF16),
             pltpu.VMEM((groups, SX, SY, GB, SZ), F32),
             pltpu.VMEM((2 * bands, ROWS * SZ), BF16),

time: 72.9 us -> 72.7 us (level)
  no operation moved by 1% of the time
where the time goes in v4:
time: 72.7 us; the launch traced here: 72.6 us
  Pallas kernels  69.9 us (96%)
  local copies, waits for them, and re-layouts  1.39 us (2%)
  between operations  1.29 us (2%)
    pallas_call x1, Pallas kernels, per_device(): pl.pallas_call(functools.partial(kernel, tiles), out_shape=(jax.ShapeDtyp...  69.9 us

profile of v4, /device:TPU:1, one launch (start us, length us, event | category | flops | bytes accessed | tf_op | source)
XLA Modules:
  0.0 72.6 jit_solution(13470014425714710134)
XLA Ops:
  1.3 69.9 %filter.1 = (f32[16,64,128]{2,1,0:T(8,128)S(1)}, f32[16,32]{1,0:T(8,128)S(1)}) custom-call(f32[16,64,128]{2,1,0:T(8,128)} %bitcast.12, f32[64,128]{1,0:T(8,128)} %bitcast.14, f32[32,16,128]{2,1,0:T(8,128)} %bitcast.13, f32[16,32]{1,0:T(8,128)} %bitcast.16, s32[1]{0:T(128)S(6)} %copy.12.slot_live, s32[32]{0:T(128)} %bitcast.17, s32[32,128]{1,0:T(8,128)} %bitcast.15), custom_call_target="tpu_custom_call" | custom-call | tf_op jit(solution)/shard_map/filter/pallas_call | solution.py:493
  71.2 0.8 %copy.13 = f32[16,1,8,8,128]{4,3,2,1,0:T(8,128)} copy(f32[16,1,8,8,128]{4,3,2,1,0:T(8,128)S(1)} %bitcast.11) | data formatting | bytes 1048576
  72.0 0.6 copy.14
